TPU v7x, 32 devices: a whole 2x2x4 slice. The times are simulated.
32 devices in a mesh: cells: 8 (over z, x), genes: 4 (over y, core).
Axes of the slice: x: 2, y: 2, z: 4, core: 2. Of those that a mesh axis runs over, the one named last changes fastest.
Arguments:
- counts: int32 [2000, 49152], P('genes', 'cells'), may hold values from 0 to 21, as said below
- start_basis: float32 [2000, 64], P('genes'), may hold values from -6 to 6
Outputs:
- embeddings: float32 [49152, 64], P(('cells', 'genes'))
Inputs may be any that keep to these rules, and one draw needn't show every extreme that they name: `counts`: every cell has at least one nonzero count.
All inputs are finite; a program needn't handle non-finite values.
Results may differ from a plain program's by a relative error of at most 0.00015.
Values sent between devices are 32-bit elements; how exact they have to be, the bound alone decides.
A program may use at most 128 MiB of HBM per device.

v0:
```python
import math

import jax
import jax.numpy as jnp
from jax import lax
from jax.sharding import PartitionSpec as P

ITERS = 2


epsilon = 1e-05
clip_top = 10.0
highest = lax.Precision.HIGHEST


def partner(value, axis, stride):
    mask = 2**stride
    pairs = [(source, source ^ mask) for source in range(lax.axis_size(axis))]
    return lax.ppermute(value, axis, pairs)


def shards(counts, start_basis):
    genes_dev, cells_dev = counts.shape
    groups = lax.axis_size("genes")
    cell_devs = lax.axis_size("cells")
    share_rows = cells_dev // groups
    half_devs = cell_devs // 2
    half_bits = half_devs.bit_length() - 1
    set_cells = cells_dev * half_devs
    dataset = lax.axis_index("cells") // half_devs
    select = (jnp.arange(2) == dataset).astype(jnp.float32)
    raw_counts = counts.astype(jnp.float32)
    totals = lax.psum(jnp.sum(raw_counts, axis=0), "genes")
    lognorm = jnp.log1p(10000.0 * raw_counts / totals[None, :])
    local_sum = jnp.sum(lognorm, axis=1)
    gene_sums = lax.psum(select[:, None] * local_sum[None, :], "cells")
    center = jnp.sum(select[:, None] * gene_sums, axis=0) / set_cells
    centered = lognorm - center[:, None]
    gene_squares = lax.psum(
        select[:, None] * jnp.sum(centered * centered, axis=1)[None, :], "cells"
    )
    spread = jnp.sum(select[:, None] * gene_squares, axis=0) / set_cells
    deviation = jnp.sqrt(spread + epsilon)
    scaled = jnp.minimum((lognorm - center[:, None]) / deviation[:, None], clip_top)

    def gram_local(matrix):
        return jnp.dot(matrix.T, matrix, precision=highest)

    def set_gram(partial_gram):
        running = partial_gram
        for bit_index in range(half_bits):
            running = running + partner(running, "cells", bit_index)
        return running

    def orthonormal_rows(weight):
        partial_rows = lax.dot_general(scaled, weight, (((0,), (0,)), ((), ())), precision=highest)
        row_block = lax.psum(partial_rows, "genes")
        device_gram = gram_local(row_block)
        gram_set = set_gram(device_gram)
        factor = jnp.linalg.cholesky(gram_set)
        return jax.scipy.linalg.solve_triangular(factor, row_block.T, lower=True).T

    basis = orthonormal_rows(start_basis)
    for sweep_index in range(ITERS):
        other_running = jnp.dot(scaled, basis, precision=highest)
        for other_bit_index in range(half_bits):
            other_running = other_running + partner(other_running, "cells", other_bit_index)
        basis = orthonormal_rows(partner(other_running, "cells", cell_devs.bit_length() - 2))
    return lax.dynamic_slice_in_dim(
        basis, lax.axis_index("genes") * share_rows, share_rows, 0
    ) * math.sqrt(set_cells)


def solution(mesh):
    placed = (P("genes", "cells"), P("genes", None))
    return jax.shard_map(
        shards, mesh=mesh, in_specs=placed, out_specs=P(("cells", "genes"), None), check_vma=False
    )
```

profile of v0, /device:TPU:0, one launch (start us, length us, event | category | flops | bytes accessed | tf_op | source)
XLA Modules:
  0.0 412.5 jit_solution(12970784951077219681)
XLA Ops:
  6.5 5.9 %convert_reduce_fusion = f32[6144]{0:T(1024)S(1)} fusion(s32[500,6144]{1,0:T(8,128)} %param.5), kind=kLoop, calls=%fused_computation.3 | loop fusion | flops 6137856 | bytes 12312576 | tf_op jit(solution)/shard_map/reduce_sum | solution.py:33
  12.5 12.9 %psum.42 = f32[6144]{0:T(1024)S(1)} all-reduce(f32[6144]{0:T(1024)S(1)} %convert_reduce_fusion), channel_id=1, replica_groups=mesh['cells'=8,'genes'=4] {'genes'}, use_global_device_ids=true, to_apply=%region_1.2 | all-reduce | flops 6144 | bytes 49152 | tf_op jit(solution)/shard_map/psum | solution.py:33
  25.3 9.8 %fusion.19 = f32[500]{0:T(512)S(1)} fusion(f32[6144]{0:T(1024)S(1)} %psum.42, s32[500,6144]{1,0:T(8,128)} %param.5), kind=kLoop, calls=%fused_computation.43 | loop fusion | flops 12287500 | bytes 12314576 | tf_op jit(solution)/shard_map/reduce_sum | solution.py:35
  35.2 21.8 %psum.43 = f32[2,500]{1,0:T(2,128)S(1)} all-reduce(f32[2,500]{1,0:T(2,128)S(1)} %broadcast_multiply_fusion.1), channel_id=1, replica_groups=mesh['cells'=8,'genes'=4] {'cells'}, use_global_device_ids=true, to_apply=%region_3.4 | all-reduce | flops 1000 | bytes 8000 | tf_op jit(solution)/shard_map/psum | solution.py:36
  57.1 10.6 %multiply_reduce_fusion = f32[500]{0:T(512)S(1)} fusion(f32[500]{0:T(512)S(1)} %broadcast_multiply_fusion.2, f32[6144]{0:T(1024)S(1)} %psum.42, s32[500,6144]{1,0:T(8,128)} %param.5), kind=kLoop, calls=%fused_computation.1 | loop fusion | flops 18431500 | bytes 12316576 | tf_op jit(solution)/shard_map/reduce_sum | solution.py:40
  67.8 17.5 %psum.44 = f32[2,500]{1,0:T(2,128)S(1)} all-reduce(f32[2,500]{1,0:T(2,128)S(1)} %broadcast_multiply_fusion), channel_id=1, replica_groups=mesh['cells'=8,'genes'=4] {'cells'}, use_global_device_ids=true, to_apply=%region_6.7 | all-reduce | flops 1000 | bytes 8000 | tf_op jit(solution)/shard_map/psum | solution.py:39
  85.4 8.6 %divide_minimum_fusion = f32[500,6144]{1,0:T(8,128)S(1)} fusion(f32[500]{0:T(512)S(1)} %add_sqrt_fusion, f32[500]{0:T(512)S(1)} %broadcast_multiply_fusion.2, f32[6144]{0:T(1024)S(1)} %psum.42, s32[500,6144]{1,0:T(8,128)} %param.5), kind=kLoop, calls=%fused_computation | loop fusion | flops 18432000 | bytes 24604576 | tf_op jit(solution)/shard_map/min | solution.py:44
  94.0 4.5 %copy-done.1 = f32[500,6144]{1,0:T(8,128)} copy-done((f32[500,6144]{1,0:T(8,128)}, f32[500,6144]{1,0:T(8,128)S(1)}, u32[]{:S(2)}) %copy-start.1) | copy-done | bytes 12288024
  98.5 10.1 %fusion.20 = f32[6144,64]{0,1:T(8,128)} fusion(f32[500,6144]{1,0:T(8,128)S(1)} %divide_minimum_fusion, f32[500,64]{0,1:T(8,128)S(1)} %copy-done), kind=kOutput, calls=%fused_computation.44 | convolution fusion | flops 2359296000 | bytes 13988864 | tf_op jit(solution)/shard_map/dot_general | solution.py:56
  108.9 40.6 %all-reduce.4.cloned.1.call-done = f32[6144,64]{0,1:T(8,128)} async-done(((f32[6144,64]{0,1:T(8,128)}), f32[6144,64]{0,1:T(8,128)}) %all-reduce.4.cloned.1.call-update) | async-done | bytes 1572880 | tf_op jit(solution)/shard_map/psum | solution.py:57
  149.5 3.3 fusion.21
  160.8 5.8 %cholesky.59 = f32[64,64]{1,0:T(8,128)S(1)} custom-call(f32[64,64]{1,0:T(8,128)S(1)} %fusion.14), custom_call_target="Cholesky" | custom-call | tf_op jit(solution)/shard_map/jit(cholesky)/cholesky | solution.py:60
  168.0 4.9 %custom-call.7 = f32[1,64,64]{1,2,0:T(8,128)S(1)} custom-call(f32[1,64,64]{2,1,0:T(8,128)S(1)} %fusion.6), custom_call_target="InvertDiagBlocksLowerTriangular" | custom-call | tf_op jit(solution)/shard_map/jit(_solve_triangular)/triangular_solve | solution.py:61
  172.9 2.9 fusion.4
  175.8 14.2 %fusion.22 = f32[500,64]{0,1:T(8,128)S(1)} fusion(f32[500,6144]{1,0:T(8,128)} %copy-done.1, f32[64,6144]{1,0:T(8,128)S(1)} %fusion.4), kind=kOutput, calls=%fused_computation.46 | convolution fusion | flops 2359296000 | bytes 13988864 | tf_op jit(solution)/shard_map/dot_general | solution.py:65
  191.5 3.5 collective-permute-done.2
  196.6 4.9 %collective-permute-done.3 = f32[500,64]{0,1:T(8,128)S(1)} collective-permute-done((f32[500,64]{0,1:T(8,128)S(1)}, f32[500,64]{0,1:T(8,128)S(1)}, u32[]{:S(2)}, u32[]{:S(2)}) %collective-permute-start.3) | collective-permute-done | bytes 128032 | tf_op jit(solution)/shard_map/ppermute | solution.py:19
  203.1 5.7 %collective-permute-done.4 = f32[500,64]{0,1:T(8,128)S(1)} collective-permute-done((f32[500,64]{0,1:T(8,128)S(1)}, f32[500,64]{0,1:T(8,128)S(1)}, u32[]{:S(2)}, u32[]{:S(2)}) %collective-permute-start.4) | collective-permute-done | bytes 128032 | tf_op jit(solution)/shard_map/ppermute | solution.py:19
  208.8 12.3 %fusion.23 = f32[6144,64]{0,1:T(8,128)} fusion(f32[500,6144]{1,0:T(8,128)} %copy-done.1, f32[500,64]{0,1:T(8,128)S(1)} %collective-permute-done.4), kind=kOutput, calls=%fused_computation.47 | convolution fusion | flops 2359296000 | bytes 13988864 | tf_op jit(solution)/shard_map/dot_general | solution.py:56
  221.4 42.2 %all-reduce.6.cloned.1.call-done = f32[6144,64]{0,1:T(8,128)} async-done(((f32[6144,64]{0,1:T(8,128)}), f32[6144,64]{0,1:T(8,128)}) %all-reduce.6.cloned.1.call-update) | async-done | bytes 1572880 | tf_op jit(solution)/shard_map/psum | solution.py:57
  263.6 3.3 fusion.24
  275.0 5.8 %cholesky.70 = f32[64,64]{1,0:T(8,128)S(1)} custom-call(f32[64,64]{1,0:T(8,128)S(1)} %fusion.12), custom_call_target="Cholesky" | custom-call | tf_op jit(solution)/shard_map/jit(cholesky)/cholesky | solution.py:60
  282.2 4.9 %custom-call.8 = f32[1,64,64]{1,2,0:T(8,128)S(1)} custom-call(f32[1,64,64]{2,1,0:T(8,128)S(1)} %fusion.7), custom_call_target="InvertDiagBlocksLowerTriangular" | custom-call | tf_op jit(solution)/shard_map/jit(_solve_triangular)/triangular_solve | solution.py:61
  289.9 14.4 %fusion.25 = f32[500,64]{0,1:T(8,128)S(1)} fusion(f32[500,6144]{1,0:T(8,128)} %copy-done.1, f32[64,6144]{1,0:T(8,128)S(1)} %fusion.2), kind=kOutput, calls=%fused_computation.49 | convolution fusion | flops 2359296000 | bytes 13988864 | tf_op jit(solution)/shard_map/dot_general | solution.py:65
  305.9 3.5 collective-permute-done.7
  311.0 4.9 %collective-permute-done.8 = f32[500,64]{0,1:T(8,128)S(1)} collective-permute-done((f32[500,64]{0,1:T(8,128)S(1)}, f32[500,64]{0,1:T(8,128)S(1)}, u32[]{:S(2)}, u32[]{:S(2)}) %collective-permute-start.8) | collective-permute-done | bytes 128032 | tf_op jit(solution)/shard_map/ppermute | solution.py:19
  317.5 5.7 %collective-permute-done.9 = f32[500,64]{0,1:T(8,128)S(1)} collective-permute-done((f32[500,64]{0,1:T(8,128)S(1)}, f32[500,64]{0,1:T(8,128)S(1)}, u32[]{:S(2)}, u32[]{:S(2)}) %collective-permute-start.9) | collective-permute-done | bytes 128032 | tf_op jit(solution)/shard_map/ppermute | solution.py:19
  323.2 12.7 %fusion.26 = f32[6144,64]{0,1:T(8,128)} fusion(f32[500,6144]{1,0:T(8,128)} %copy-done.1, f32[500,64]{0,1:T(8,128)S(1)} %collective-permute-done.9), kind=kOutput, calls=%fused_computation.50 | convolution fusion | flops 2359296000 | bytes 13988864 | tf_op jit(solution)/shard_map/dot_general | solution.py:56
  335.9 42.5 %all-reduce.8.cloned.1.call-done = f32[6144,64]{0,1:T(8,128)} async-done(((f32[6144,64]{0,1:T(8,128)}), f32[6144,64]{0,1:T(8,128)}) %all-reduce.8.cloned.1.call-update) | async-done | bytes 1572880 | tf_op jit(solution)/shard_map/psum | solution.py:57
  378.4 3.3 fusion.27
  389.7 5.8 %cholesky.81 = f32[64,64]{1,0:T(8,128)S(1)} custom-call(f32[64,64]{1,0:T(8,128)S(1)} %fusion.10), custom_call_target="Cholesky" | custom-call | tf_op jit(solution)/shard_map/jit(cholesky)/cholesky | solution.py:60
  396.9 4.9 %custom-call.9 = f32[1,64,64]{1,2,0:T(8,128)S(1)} custom-call(f32[1,64,64]{2,1,0:T(8,128)S(1)} %fusion.8), custom_call_target="InvertDiagBlocksLowerTriangular" | custom-call | tf_op jit(solution)/shard_map/jit(_solve_triangular)/triangular_solve | solution.py:61
  (62 shorter events, 44.9 us)
Async XLA Ops:
  6.5 92.0 %copy-start = (f32[500,64]{0,1:T(8,128)S(1)}, f32[500,64]{0,1:T(8,128)}, u32[]{:S(2)}) copy-start(f32[500,64]{0,1:T(8,128)} %param.6) | copy-start | bytes 384004
  6.5 142.9 %all-reduce.4.cloned.1.call-start = ((), (), s32[]{:S(2)}) async-start(), calls=%async_computation | async-start | bytes 3145728 | tf_op jit(solution)/shard_map/psum | solution.py:57
  94.0 4.5 %copy-start.1 = (f32[500,6144]{1,0:T(8,128)}, f32[500,6144]{1,0:T(8,128)S(1)}, u32[]{:S(2)}) copy-start(f32[500,6144]{1,0:T(8,128)S(1)} %divide_minimum_fusion) | copy-start | bytes 36864004
  108.7 154.9 %all-reduce.6.cloned.1.call-start = ((), (), s32[]{:S(2)}) async-start(), calls=%async_computation.1 | async-start | bytes 3145728 | tf_op jit(solution)/shard_map/psum | solution.py:57
  152.8 4.0 collective-permute-start
  156.8 3.9 collective-permute-start.1
  190.0 5.0 %collective-permute-start.2 = (f32[500,64]{0,1:T(8,128)S(1)}, f32[500,64]{0,1:T(8,128)S(1)}, u32[]{:S(2)}, u32[]{:S(2)}) collective-permute-start(f32[500,64]{0,1:T(8,128)S(1)} %fusion.22), channel_id=1, source_target_pairs={{0,4},{4,0},{8,12},{12,8},{16,20},{20,16},{24,28},{28,24},{1,5},{5... | collective-permute-start | bytes 384008 | tf_op jit(solution)/shard_map/ppermute | solution.py:19
  195.0 6.4 %collective-permute-start.3 = (f32[500,64]{0,1:T(8,128)S(1)}, f32[500,64]{0,1:T(8,128)S(1)}, u32[]{:S(2)}, u32[]{:S(2)}) collective-permute-start(f32[500,64]{0,1:T(8,128)S(1)} %add.69), channel_id=1, source_target_pairs={{0,8},{4,12},{8,0},{12,4},{16,24},{20,28},{24,16},{28,20},{1,9},{5... | collective-permute-start | bytes 384008 | tf_op jit(solution)/shard_map/ppermute | solution.py:19
  201.5 7.3 %collective-permute-start.4 = (f32[500,64]{0,1:T(8,128)S(1)}, f32[500,64]{0,1:T(8,128)S(1)}, u32[]{:S(2)}, u32[]{:S(2)}) collective-permute-start(f32[500,64]{0,1:T(8,128)S(1)} %add.70), channel_id=1, source_target_pairs={{0,16},{4,20},{8,24},{12,28},{16,0},{20,4},{24,8},{28,12},{1,17},{... | collective-permute-start | bytes 384008 | tf_op jit(solution)/shard_map/ppermute | solution.py:19
  221.2 157.2 %all-reduce.8.cloned.1.call-start = ((), (), s32[]{:S(2)}) async-start(), calls=%async_computation.2 | async-start | bytes 3145728 | tf_op jit(solution)/shard_map/psum | solution.py:57
  267.0 4.0 collective-permute-start.5
  270.9 3.9 collective-permute-start.6
  304.4 5.0 %collective-permute-start.7 = (f32[500,64]{0,1:T(8,128)S(1)}, f32[500,64]{0,1:T(8,128)S(1)}, u32[]{:S(2)}, u32[]{:S(2)}) collective-permute-start(f32[500,64]{0,1:T(8,128)S(1)} %fusion.25), channel_id=1, source_target_pairs={{0,4},{4,0},{8,12},{12,8},{16,20},{20,16},{24,28},{28,24},{1,5},{5... | collective-permute-start | bytes 384008 | tf_op jit(solution)/shard_map/ppermute | solution.py:19
  309.4 6.4 %collective-permute-start.8 = (f32[500,64]{0,1:T(8,128)S(1)}, f32[500,64]{0,1:T(8,128)S(1)}, u32[]{:S(2)}, u32[]{:S(2)}) collective-permute-start(f32[500,64]{0,1:T(8,128)S(1)} %add.73), channel_id=1, source_target_pairs={{0,8},{4,12},{8,0},{12,4},{16,24},{20,28},{24,16},{28,20},{1,9},{5... | collective-permute-start | bytes 384008 | tf_op jit(solution)/shard_map/ppermute | solution.py:19
  315.9 7.3 %collective-permute-start.9 = (f32[500,64]{0,1:T(8,128)S(1)}, f32[500,64]{0,1:T(8,128)S(1)}, u32[]{:S(2)}, u32[]{:S(2)}) collective-permute-start(f32[500,64]{0,1:T(8,128)S(1)} %add.74), channel_id=1, source_target_pairs={{0,16},{4,20},{8,24},{12,28},{16,0},{20,4},{24,8},{28,12},{1,17},{... | collective-permute-start | bytes 384008 | tf_op jit(solution)/shard_map/ppermute | solution.py:19
  381.7 4.0 collective-permute-start.10
  385.7 3.9 collective-permute-start.11
Sparse Core Ops, SparseCore 0:
  108.8 40.6 all-reduce.3
  221.3 42.2 all-reduce.5
  336.0 42.2 all-reduce.7
where the time goes:
time: 419 us; the launch traced here: 412 us
  waiting for transfers between devices  168 us (40%)
  matrix products  82.3 us (20%)
  other arithmetic  72.3 us (17%)
  blocking collectives  52.2 us (12%)
  starting transfers between devices  19 us (5%)
  between operations  13.8 us (3%)
  local copies, waits for them, and re-layouts  4.74 us (1%)
    psum x3, waiting for transfers between devices, orthonormal_rows(): row_block = lax.psum(partial_rows, 'genes')  125 us
    ppermute x12, waiting for transfers between devices, partner(): return lax.ppermute(value, axis, pairs)  42.8 us
    dot_general x3, matrix products, orthonormal_rows(): lax.dot_general(scaled, weight, (((0,), (0,)), ((), ())), precision=highest)  35.1 us
    dot_general x2, matrix products, shards(): other_running = jnp.dot(scaled, basis, precision=highest)  28.6 us
    psum x1, blocking collectives, shards(): gene_sums = lax.psum(select[:, None] * local_sum[None, :], 'cells')  21.8 us
    another operation x9, other arithmetic, orthonormal_rows(): factor = jnp.linalg.cholesky(gram_set)  19.6 us
    ppermute x12, starting transfers between devices, partner(): return lax.ppermute(value, axis, pairs)  18.5 us
    psum x1, blocking collectives, shards(): lax.psum(select[:, None] * jnp.sum(centered * centered, axis=1)[None, :],...  17.5 us
  transfers between devices with their start and end apart: 15, of which 15 were waited for; matrix products, arithmetic and copies ran while one was open for 0% of the time, Pallas kernels for 0%

commit v1 on v0

v1 whole, which is shorter than its diff:
```python
import functools
import math

import jax
import jax.numpy as jnp
from jax import lax
from jax.experimental import pallas as pl
from jax.experimental.pallas import tpu as pltpu
from jax.sharding import PartitionSpec as P

ITERS = 2
epsilon = 1e-05
clip_top = 10.0
highest = lax.Precision.HIGHEST
f32 = jnp.float32
bf16 = jnp.bfloat16
LANES = 128
NT = (((1,), (1,)), ((), ()))


def split_two(value):
    high = value.astype(bf16)
    return high, (value - high.astype(f32)).astype(bf16)


def split_three(value):
    high = value.astype(bf16)
    rest = value - high.astype(f32)
    middle, low = split_two(rest)
    return high, middle, low


def inverse_factor(gram_folded):
    half_rows = gram_folded.shape[0]
    rank = 2 * half_rows
    lane = lax.broadcasted_iota(jnp.int32, (rank, 2 * rank), 1)
    row = lax.broadcasted_iota(jnp.int32, (rank, 2 * rank), 0)
    row_column = lax.broadcasted_iota(jnp.int32, (rank, 1), 0)
    gram = jnp.concatenate([gram_folded, pltpu.roll(gram_folded, rank, 1)], axis=0)
    both = jnp.where(lane < rank, gram, jnp.where(lane == row + rank, 1.0, 0.0))

    def step(k, both):
        pivot_row = jnp.sum(jnp.where(row == k, both, 0.0), axis=0, keepdims=True)
        column = jnp.sum(jnp.where(lane == k, both, 0.0), axis=1, keepdims=True)
        pivot = jnp.sum(jnp.where(row_column == k, column, 0.0), axis=0, keepdims=True)
        factor = jnp.where(row_column > k, column / pivot, 0.0)
        return both - factor * pivot_row

    both = lax.fori_loop(0, rank, step, both)
    diagonal = jnp.sum(jnp.where(lane == row, both, 0.0), axis=1, keepdims=True)
    return both[:, rank:] * lax.rsqrt(diagonal)


def kernel(
    cfg, counts_ref, basis_ref, out_ref,
    cnt, logs, xhi, xlo, tot, acc, center_ref, scale_ref, stat, wsplit,
    send_a, recv_a, send_b, recv_b, own_p, recv_p, product, gram_acc, inverse,
    shares, quarter_out, quarter_in, whole, gram_g, gram_c,
    load_sem, tot_sem, stat_sem, a_sem, b_send, b_recv, c_sem, rs_sem, x_sem, ag_sem, gg_sem, gc_sem,
):
    genes_dev, cells_dev, rank, groups, cell_devs, chunk, share_rows = cfg
    half_devs = cell_devs // 2
    set_cells = cells_dev * half_devs
    quarter = cells_dev // groups
    per_quarter = quarter // chunk
    steps = 2 * per_quarter
    gene = lax.axis_index("genes")
    cell = lax.axis_index("cells")
    y, core = gene // 2, gene % 2
    core_mate = {"genes": y * 2 + 1 - core}
    y_mate = {"genes": (1 - y) * 2 + core}
    dataset = cell // half_devs
    place = cell % half_devs
    cross = {"cells": (1 - dataset) * half_devs + place}

    def gene_peer(i):
        return {"genes": (gene + i) % groups}

    def set_place(i):
        return (place + i) % half_devs

    def set_peer(i):
        return {"cells": dataset * half_devs + set_place(i)}

    def remote(src, dst, send, recv, device):
        return pltpu.make_async_remote_copy(
            src_ref=src, dst_ref=dst, send_sem=send, recv_sem=recv,
            device_id=device, device_id_type=pl.DeviceIdType.MESH,
        )

    load_cols = cells_dev // 6 if cells_dev % (6 * LANES) == 0 else cells_dev
    loads = []
    for i in range(cells_dev // load_cols):
        cols = pl.ds(i * load_cols, load_cols)
        copy = pltpu.make_async_copy(counts_ref.at[:, cols], cnt.at[:, cols], load_sem.at[i])
        copy.start()
        loads.append(copy)

    barrier = pltpu.get_barrier_semaphore()
    mates = [gene_peer(i) for i in range(1, groups)]
    mates += [set_peer(i) for i in range(1, half_devs)] + [cross]
    for mate in mates:
        pl.semaphore_signal(barrier, inc=1, device_id=mate, device_id_type=pl.DeviceIdType.MESH)

    acc[...] = jnp.zeros_like(acc)
    stat[0] = jnp.zeros(stat.shape[1:], f32)
    for i, piece in enumerate(split_three(basis_ref[...])):
        wsplit[i * rank : (i + 1) * rank, :] = piece

    for i, copy in enumerate(loads):
        copy.wait()

        def add_genes(j, carry, base=i * load_cols):
            cols = pl.ds(pl.multiple_of(base + j * LANES, LANES), LANES)
            tot[0, :, cols] = jnp.sum(cnt[:, cols], axis=0, keepdims=True).astype(f32)
            return carry

        lax.fori_loop(0, load_cols // LANES, add_genes, 0)
    pl.semaphore_wait(barrier, len(mates))
    copies = [
        remote(tot.at[0], tot.at[i], tot_sem.at[0, i], tot_sem.at[1, i], gene_peer(i))
        for i in range(1, groups)
    ]
    for copy in copies:
        copy.start()
    for copy in copies:
        copy.wait()

    def to_logs(j, carry):
        cols = pl.ds(pl.multiple_of(j * LANES, LANES), LANES)
        total = tot[0, :, cols]
        for i in range(1, groups):
            total = total + tot[i, :, cols]
        value = jnp.log(1.0 + cnt[:, cols].astype(f32) * (10000.0 / total))
        logs[:, cols] = value
        acc[0:genes_dev, :] += value
        return carry

    lax.fori_loop(0, cells_dev // LANES, to_logs, 0)
    stat[0, 0:1, :] = jnp.sum(acc[...].T, axis=0, keepdims=True)
    center_ref[...] = jnp.broadcast_to(
        jnp.sum(acc[...], axis=1, keepdims=True) * (1.0 / cells_dev), center_ref.shape
    )
    acc[...] = jnp.zeros_like(acc)

    def add_squares(j, carry):
        cols = pl.ds(pl.multiple_of(j * LANES, LANES), LANES)
        centered = logs[:, cols] - center_ref[0:genes_dev, :]
        acc[0:genes_dev, :] += centered * centered
        return carry

    lax.fori_loop(0, cells_dev // LANES, add_squares, 0)
    stat[0, 1:2, :] = jnp.sum(acc[...].T, axis=0, keepdims=True)
    copies = [
        remote(stat.at[0], stat.at[i], stat_sem.at[0, i], stat_sem.at[1, i], set_peer(i))
        for i in range(1, half_devs)
    ]
    for copy in copies:
        copy.start()
    for copy in copies:
        copy.wait()
    gene_sum = stat[0, 0:1, :]
    for i in range(1, half_devs):
        gene_sum = gene_sum + stat[i, 0:1, :]
    center = gene_sum * (1.0 / set_cells)
    squares = jnp.zeros_like(center)
    for i in range(half_devs):
        shift = stat[i, 0:1, :] * (1.0 / cells_dev) - center
        squares = squares + (stat[i, 1:2, :] + cells_dev * (shift * shift))
    scale = 1.0 / jnp.sqrt(squares * (1.0 / set_cells) + epsilon)
    wide = (LANES, center.shape[1])
    center_ref[...] = jnp.broadcast_to(center, wide).T
    scale_ref[...] = jnp.broadcast_to(scale, wide).T

    def offset(k, half):
        return pl.multiple_of(
            (k // per_quarter) * (2 * quarter) + half * quarter + (k % per_quarter) * chunk, LANES
        )

    def scale_chunk(start):
        def part(j, carry):
            cols = pl.ds(pl.multiple_of(start + j * LANES, LANES), LANES)
            value = (logs[:, cols] - center_ref[0:genes_dev, :]) * scale_ref[0:genes_dev, :]
            high, low = split_two(jnp.minimum(value, clip_top))
            xhi[:, cols] = high
            xlo[:, cols] = low
            return carry

        lax.fori_loop(0, chunk // LANES, part, 0)

    def project(start):
        cols = pl.ds(start, chunk)
        top = jnp.dot(wsplit[...], xhi[:, cols], preferred_element_type=f32)
        rest = jnp.dot(wsplit[0 : 2 * rank, :], xlo[:, cols], preferred_element_type=f32)
        small = top[2 * rank :] + rest[rank:]
        return top[0:rank] + (top[rank : 2 * rank] + rest[0:rank] + small)

    def copy_a(k):
        return remote(send_a.at[k], recv_a.at[k], a_sem.at[0, k], a_sem.at[1, k], core_mate)

    def copy_c(k):
        return remote(own_p.at[k], recv_p.at[k], c_sem.at[0, k], c_sem.at[1, k], core_mate)

    def copy_b(stage, k, slot):
        return remote(
            send_b.at[k], recv_b.at[stage, slot], b_send.at[slot], b_recv.at[stage, slot], y_mate
        )

    def chip_sum(k, first):
        other = offset(k, 1 - core)
        if first:
            scale_chunk(other)
        send_a[k] = project(other)
        copy_a(k).start()
        mine = offset(k, core)
        if first:
            scale_chunk(mine)
        value = project(mine)
        copy_a(k).wait_recv()
        send_b[k] = value + recv_a[k]

    def add_gram(pieces):
        gram_acc[...] += lax.dot_general(pieces, pieces, NT, preferred_element_type=f32)

    def pieces_of(value):
        return jnp.concatenate(split_two(value), axis=0)

    def add_product(value, start):
        cols = pl.ds(start, chunk)
        pieces = pieces_of(value)
        product[0:genes_dev, :] += lax.dot_general(
            xhi[:, cols], pieces, NT, preferred_element_type=f32
        ) + lax.dot_general(xlo[:, cols], pieces, NT, preferred_element_type=f32)
        add_gram(pieces)

    lane_g = lax.broadcasted_iota(jnp.int32, (rank // 2, 2 * rank), 1)

    def folded_gram():
        gram = gram_acc[0:rank, :] + gram_acc[rank:, :]
        gram = gram + pltpu.roll(gram, rank, 1)
        return jnp.where(lane_g < rank, gram[0 : rank // 2], gram[rank // 2 :])

    fold = product.shape[0] // 2
    last = ITERS
    for stage in range(ITERS):
        def first_loop(k, carry, stage=stage):
            chip_sum(k, stage == 0)
            copy_b(stage, k, k).start()
            return carry

        lax.fori_loop(0, steps, first_loop, 0)
        product[...] = jnp.zeros_like(product)
        gram_acc[...] = jnp.zeros_like(gram_acc)
        if stage > 0:
            inverse[...] = inverse_factor(whole[stage - 1, fold : fold + rank // 2, :])

        def second_loop(k, carry, stage=stage):
            copy_b(stage, k, k).wait()
            value = send_b[k] + recv_b[stage, k]
            if stage > 0:
                value = jnp.dot(inverse[...], value, precision=highest, preferred_element_type=f32)
            own_p[k] = value
            copy_c(k).start()
            add_product(value, offset(k, core))
            copy_a(k).wait_send()
            copy_c(k).wait()
            add_product(recv_p[k], offset(k, 1 - core))
            return carry

        lax.fori_loop(0, steps, second_loop, 0)

        lane = lax.broadcasted_iota(jnp.int32, (fold, 2 * rank), 1)
        summed = product[...] + pltpu.roll(product[...], rank, 1)
        local = whole.at[ITERS + stage]
        local[0:fold, :] = jnp.where(lane < rank, summed[0:fold], summed[fold:])
        local[fold : fold + rank // 2, :] = folded_gram()
        if local.shape[0] > fold + rank // 2:
            rest = local.shape[0] - fold - rank // 2
            local[fold + rank // 2 :, :] = jnp.zeros((rest, 2 * rank), f32)

        def rows_of(index):
            return pl.ds(pl.multiple_of(index * share_rows, 8), share_rows)

        copies = [
            remote(
                local.at[rows_of(set_place(i))], shares.at[stage, i],
                rs_sem.at[0, stage, i], rs_sem.at[1, stage, i], set_peer(i),
            )
            for i in range(1, half_devs)
        ]
        for copy in copies:
            copy.start()
        for copy in copies:
            copy.wait()
        value = local[rows_of(place), :]
        for i in range(1, half_devs):
            value = value + shares[stage, i]
        quarter_out[stage] = value
        copy = remote(
            quarter_out.at[stage], quarter_in.at[stage], x_sem.at[0, stage], x_sem.at[1, stage], cross
        )
        copy.start()
        copy.wait()
        mine = rows_of(place)
        copies = [
            remote(
                quarter_in.at[stage], whole.at[stage, mine],
                ag_sem.at[0, stage, i], ag_sem.at[1, stage, i], set_peer(i),
            )
            for i in range(1, half_devs)
        ]
        for copy in copies:
            copy.start()
        whole[stage, mine, :] = quarter_in[stage]
        for copy in copies:
            copy.wait()
        turned = whole[stage, 0:fold, :].T
        for part, rows in ((0, turned[0:rank]), (1, turned[rank:])):
            width = min(fold, genes_dev - part * fold)
            for i, piece in enumerate(split_three(rows[:, 0:width])):
                wsplit[i * rank : (i + 1) * rank, part * fold : part * fold + width] = piece

    def send_loop(j, carry):
        k = (1 - y) * per_quarter + j
        chip_sum(k, False)
        copy_b(last, k, j).start()
        return carry

    lax.fori_loop(0, per_quarter, send_loop, 0)

    def keep_loop(j, carry):
        chip_sum(y * per_quarter + j, False)
        return carry

    lax.fori_loop(0, per_quarter, keep_loop, 0)
    gram_acc[...] = jnp.zeros_like(gram_acc)
    inverse[...] = inverse_factor(whole[ITERS - 1, fold : fold + rank // 2, :])

    def last_loop(j, carry):
        copy_b(last, y * per_quarter + j, j).wait()
        value = send_b[y * per_quarter + j] + recv_b[last, j]
        value = jnp.dot(inverse[...], value, precision=highest, preferred_element_type=f32)
        own_p[j] = value
        add_gram(pieces_of(value))
        copy_a(j).wait_send()
        copy_a(j + per_quarter).wait_send()
        return carry

    lax.fori_loop(0, per_quarter, last_loop, 0)
    gram_g[0] = folded_gram()
    copies = [
        remote(gram_g.at[0], gram_g.at[i], gg_sem.at[0, i], gg_sem.at[1, i], gene_peer(i))
        for i in range(1, groups)
    ]
    for copy in copies:
        copy.start()
    for copy in copies:
        copy.wait()
    value = gram_g[0]
    for i in range(1, groups):
        value = value + gram_g[i]
    gram_c[0] = value
    copies = [
        remote(gram_c.at[0], gram_c.at[i], gc_sem.at[0, i], gc_sem.at[1, i], set_peer(i))
        for i in range(1, half_devs)
    ]
    for copy in copies:
        copy.start()
    for copy in copies:
        copy.wait()
    for i in range(1, half_devs):
        value = value + gram_c[i]
    inverse[...] = inverse_factor(value) * math.sqrt(set_cells)
    for j in range(per_quarter):
        out_ref[:, j * chunk : (j + 1) * chunk] = jnp.dot(
            inverse[...], own_p[j], precision=highest, preferred_element_type=f32
        )


def shards(counts, start_basis):
    genes_dev, cells_dev = counts.shape
    rank = start_basis.shape[1]
    groups = lax.axis_size("genes")
    cell_devs = lax.axis_size("cells")
    assert groups == 4 and rank == 64
    half_devs = cell_devs // 2
    quarter = cells_dev // groups
    chunk = max(c for c in range(LANES, 512 + 1, LANES) if quarter % c == 0)
    steps = 2 * quarter // chunk
    padded = -(-genes_dev // 256) * 256
    rows = padded // 2 + rank // 2
    share_rows = -(-rows // (8 * half_devs)) * 8
    block = (rank, chunk)
    dma = pltpu.SemaphoreType.DMA
    scratch = [
        pltpu.VMEM((genes_dev, cells_dev), jnp.int32),
        pltpu.VMEM((genes_dev, cells_dev), f32),
        pltpu.VMEM((genes_dev, cells_dev), bf16),
        pltpu.VMEM((genes_dev, cells_dev), bf16),
        pltpu.VMEM((groups, 1, cells_dev), f32),
        pltpu.VMEM((padded, LANES), f32),
        pltpu.VMEM((padded, LANES), f32),
        pltpu.VMEM((padded, LANES), f32),
        pltpu.VMEM((half_devs, 8, padded), f32),
        pltpu.VMEM((3 * rank, genes_dev), bf16),
        pltpu.VMEM((steps,) + block, f32),
        pltpu.VMEM((steps,) + block, f32),
        pltpu.VMEM((steps,) + block, f32),
        pltpu.VMEM((ITERS + 1, steps) + block, f32),
        pltpu.VMEM((steps,) + block, f32),
        pltpu.VMEM((steps,) + block, f32),
        pltpu.VMEM((padded, 2 * rank), f32),
        pltpu.VMEM((2 * rank, 2 * rank), f32),
        pltpu.VMEM((rank, rank), f32),
        pltpu.VMEM((ITERS, half_devs, share_rows, 2 * rank), f32),
        pltpu.VMEM((ITERS, share_rows, 2 * rank), f32),
        pltpu.VMEM((ITERS, share_rows, 2 * rank), f32),
        pltpu.VMEM((2 * ITERS, share_rows * half_devs, 2 * rank), f32),
        pltpu.VMEM((groups, rank // 2, 2 * rank), f32),
        pltpu.VMEM((half_devs, rank // 2, 2 * rank), f32),
        dma((6,)),
        dma((2, groups)),
        dma((2, half_devs)),
        dma((2, steps)),
        dma((steps,)),
        dma((ITERS + 1, steps)),
        dma((2, steps)),
        dma((2, ITERS, half_devs)),
        dma((2, ITERS)),
        dma((2, ITERS, half_devs)),
        dma((2, groups)),
        dma((2, half_devs)),
    ]
    cfg = (genes_dev, cells_dev, rank, groups, cell_devs, chunk, share_rows)
    flops = 2 * 5 * 4 * genes_dev * cells_dev * rank
    turned = pl.pallas_call(
        functools.partial(kernel, cfg),
        out_shape=jax.ShapeDtypeStruct((rank, quarter), f32),
        in_specs=[pl.BlockSpec(memory_space=pl.ANY), pl.BlockSpec(memory_space=pltpu.VMEM)],
        out_specs=pl.BlockSpec(memory_space=pltpu.VMEM),
        scratch_shapes=scratch,
        compiler_params=pltpu.CompilerParams(
            collective_id=0, has_side_effects=True, vmem_limit_bytes=60 * 2**20
        ),
        cost_estimate=pl.CostEstimate(
            flops=flops, bytes_accessed=4 * genes_dev * cells_dev,
            transcendentals=genes_dev * cells_dev,
        ),
    )(counts, start_basis.T)
    return turned.T


def solution(mesh):
    placed = (P("genes", "cells"), P("genes", None))
    return jax.shard_map(
        shards, mesh=mesh, in_specs=placed, out_specs=P(("cells", "genes"), None), check_vma=False
    )
```

time: 419 us -> 130 us (0.31); the launches traced: 412 us -> 130 us
  waiting for transfers between devices: 168 us -> 0 us
  Pallas kernels: 0 us -> 128 us
  matrix products: 82.3 us -> 0 us
  other arithmetic: 72.3 us -> 0 us
  blocking collectives: 52.2 us -> 0 us
  starting transfers between devices: 19 us -> 0 us
  between operations: 13.8 us -> 0.01 us
    pallas_call x0 -> x1, Pallas kernels: none -> 128 us  [shards(): pl.pallas_call(functools.partial(kernel, cfg), out_shape=jax.ShapeDtypeSt...]
    psum x3 -> x0, waiting for transfers between devices: 125 us -> none  [orthonormal_rows(): row_block = lax.psum(partial_rows, 'genes')]
    dot_general x8 -> x0, matrix products: 73.7 us -> none  [the longest x3 35.1 us: orthonormal_rows(): lax.dot_general(scaled, weight, (((0,), (0,)), ((), ())), precision=highest)]
    psum x3 -> x0, blocking collectives: 52.2 us -> none  [the longest x1 21.8 us: shards(): gene_sums = lax.psum(select[:, None] * local_sum[None, :], 'cells')]
    ppermute x12 -> x0, waiting for transfers between devices: 42.8 us -> none  [partner(): return lax.ppermute(value, axis, pairs)]
    another operation x15 -> x0, other arithmetic: 36.2 us -> none  [the longest x9 19.6 us: orthonormal_rows(): factor = jnp.linalg.cholesky(gram_set)]
    reduce_sum x5 -> x0, other arithmetic: 26.5 us -> none  [the longest x1 10.6 us: shards(): jnp.sum(centered * centered, axis=1)[None, :]]
    ppermute x12 -> x0, starting transfers between devices: 18.5 us -> none  [partner(): return lax.ppermute(value, axis, pairs)]
  transfers between devices with their start and end apart: 15 -> 0, of which waited for: 15 -> 0; matrix products, arithmetic and copies ran while one was open for 0% -> 0% of each run, Pallas kernels for 0% -> 0%
where the time goes in v1:
time: 130 us
  Pallas kernels  128 us (98%)
  local copies, waits for them, and re-layouts  1.77 us (1%)
    pallas_call x1, Pallas kernels, shards(): pl.pallas_call(functools.partial(kernel, cfg), out_shape=jax.ShapeDtypeSt...  128 us

profile of v1, /device:TPU:0, one launch (start us, length us, event | category | flops | bytes accessed | tf_op | source)
XLA Modules:
  0.0 130.2 jit_solution(15710891752783103484)
XLA Ops:
  0.0 128.4 %shard_map.28 = f32[64,1536]{1,0:T(8,128)} custom-call(s32[500,6144]{1,0:T(8,128)} %counts_ref.1, f32[64,500]{1,0:T(8,128)} %bitcast.3), custom_call_target="tpu_custom_call" | custom-call | flops 7864320000 | bytes 12288000 | tf_op jit(solution)/shard_map/pallas_call | solution.py:436
  128.4 1.8 %copy.4 = f32[1536,64]{0,1:T(8,128)} copy(f32[1536,64]{0,1:T(8,128)} %bitcast.2) | data formatting | bytes 786432

commit v2 on v1

--- a/solution.py
+++ b/solution.py
@@ -15,6 +15,8 @@
 f32 = jnp.float32
 bf16 = jnp.bfloat16
 LANES = 128
+ROWS = 16
+PIVOTS = 4
 NT = (((1,), (1,)), ((), ()))
 
 
@@ -39,14 +41,33 @@
     gram = jnp.concatenate([gram_folded, pltpu.roll(gram_folded, rank, 1)], axis=0)
     both = jnp.where(lane < rank, gram, jnp.where(lane == row + rank, 1.0, 0.0))
 
-    def step(k, both):
-        pivot_row = jnp.sum(jnp.where(row == k, both, 0.0), axis=0, keepdims=True)
-        column = jnp.sum(jnp.where(lane == k, both, 0.0), axis=1, keepdims=True)
-        pivot = jnp.sum(jnp.where(row_column == k, column, 0.0), axis=0, keepdims=True)
-        factor = jnp.where(row_column > k, column / pivot, 0.0)
-        return both - factor * pivot_row
-
-    both = lax.fori_loop(0, rank, step, both)
+    def step(turn, both):
+        k = turn * PIVOTS
+        rows = [
+            jnp.sum(jnp.where(row == k + j, both, 0.0), axis=0, keepdims=True) for j in range(PIVOTS)
+        ]
+        columns = [
+            jnp.sum(jnp.where(lane == k + j, both, 0.0), axis=1, keepdims=True)
+            for j in range(PIVOTS)
+        ]
+        small = {}
+        for j in range(PIVOTS):
+            for m in range(j, PIVOTS):
+                picked = jnp.where(row_column == k + j, columns[m], 0.0)
+                small[j, m] = jnp.sum(picked, axis=0, keepdims=True)
+        for j in range(PIVOTS):
+            inverse = 1.0 / small[j, j]
+            factor = jnp.where(row_column > k + j, columns[j] * inverse, 0.0)
+            for m in range(j + 1, PIVOTS):
+                ratio = small[j, m] * inverse
+                columns[m] = columns[m] - factor * small[j, m]
+                rows[m] = rows[m] - ratio * rows[j]
+                for t in range(m, PIVOTS):
+                    small[m, t] = small[m, t] - ratio * small[j, t]
+            both = both - factor * rows[j]
+        return both
+
+    both = lax.fori_loop(0, rank // PIVOTS, step, both)
     diagonal = jnp.sum(jnp.where(lane == row, both, 0.0), axis=1, keepdims=True)
     return both[:, rank:] * lax.rsqrt(diagonal)
 
@@ -126,30 +147,62 @@
     for copy in copies:
         copy.wait()
 
-    def to_logs(j, carry):
-        cols = pl.ds(pl.multiple_of(j * LANES, LANES), LANES)
-        total = tot[0, :, cols]
-        for i in range(1, groups):
-            total = total + tot[i, :, cols]
-        value = jnp.log(1.0 + cnt[:, cols].astype(f32) * (10000.0 / total))
-        logs[:, cols] = value
-        acc[0:genes_dev, :] += value
-        return carry
-
-    lax.fori_loop(0, cells_dev // LANES, to_logs, 0)
+    total = tot[0]
+    for i in range(1, groups):
+        total = total + tot[i]
+    tot[0] = 10000.0 / total
+    blocks = genes_dev // ROWS
+    tail = blocks * ROWS
+    logs[tail:, :] = jnp.zeros((logs.shape[0] - tail, cells_dev), f32)
+
+    def over_rows(body):
+        def block(r, carry):
+            body(pl.ds(pl.multiple_of(r * ROWS, ROWS), ROWS))
+            return carry
+
+        lax.fori_loop(0, blocks, block, 0)
+        if tail < genes_dev:
+            body(pl.ds(tail, genes_dev - tail))
+
+    def folded_sum(parts):
+        while len(parts) > 1:
+            parts = [sum(parts[i : i + 2]) for i in range(0, len(parts), 2)]
+        return parts[0]
+
+    starts = range(0, cells_dev, 4 * LANES)
+
+    def to_logs(rows):
+        running = None
+        for start in starts:
+            parts = []
+            for low in range(start, start + 4 * LANES, LANES):
+                cols = pl.ds(low, LANES)
+                value = jnp.log(1.0 + cnt[rows, cols].astype(f32) * tot[0, :, cols])
+                logs[rows, cols] = value
+                parts.append(value)
+            part = folded_sum(parts)
+            running = part if running is None else running + part
+        acc[rows, :] = running
+
+    over_rows(to_logs)
     stat[0, 0:1, :] = jnp.sum(acc[...].T, axis=0, keepdims=True)
     center_ref[...] = jnp.broadcast_to(
         jnp.sum(acc[...], axis=1, keepdims=True) * (1.0 / cells_dev), center_ref.shape
     )
-    acc[...] = jnp.zeros_like(acc)
-
-    def add_squares(j, carry):
-        cols = pl.ds(pl.multiple_of(j * LANES, LANES), LANES)
-        centered = logs[:, cols] - center_ref[0:genes_dev, :]
-        acc[0:genes_dev, :] += centered * centered
-        return carry
-
-    lax.fori_loop(0, cells_dev // LANES, add_squares, 0)
+
+    def add_squares(rows):
+        center = center_ref[rows, :]
+        running = None
+        for start in starts:
+            parts = []
+            for low in range(start, start + 4 * LANES, LANES):
+                centered = logs[rows, pl.ds(low, LANES)] - center
+                parts.append(centered * centered)
+            part = folded_sum(parts)
+            running = part if running is None else running + part
+        acc[rows, :] = running
+
+    over_rows(add_squares)
     stat[0, 1:2, :] = jnp.sum(acc[...].T, axis=0, keepdims=True)
     copies = [
         remote(stat.at[0], stat.at[i], stat_sem.at[0, i], stat_sem.at[1, i], set_peer(i))
@@ -178,15 +231,18 @@
         )
 
     def scale_chunk(start):
-        def part(j, carry):
-            cols = pl.ds(pl.multiple_of(start + j * LANES, LANES), LANES)
-            value = (logs[:, cols] - center_ref[0:genes_dev, :]) * scale_ref[0:genes_dev, :]
-            high, low = split_two(jnp.minimum(value, clip_top))
-            xhi[:, cols] = high
-            xlo[:, cols] = low
+        def block(r, carry):
+            rows = pl.ds(pl.multiple_of(r * 2 * ROWS, 2 * ROWS), 2 * ROWS)
+            center, scale = center_ref[rows, :], scale_ref[rows, :]
+            for j in range(chunk // LANES):
+                cols = pl.ds(pl.multiple_of(start + j * LANES, LANES), LANES)
+                value = (logs[rows, cols] - center) * scale
+                high, low = split_two(jnp.minimum(value, clip_top))
+                xhi[rows, cols] = high
+                xlo[rows, cols] = low
             return carry
 
-        lax.fori_loop(0, chunk // LANES, part, 0)
+        lax.fori_loop(0, xhi.shape[0] // (2 * ROWS), block, 0)
 
     def project(start):
         cols = pl.ds(start, chunk)
@@ -228,7 +284,7 @@
     def add_product(value, start):
         cols = pl.ds(start, chunk)
         pieces = pieces_of(value)
-        product[0:genes_dev, :] += lax.dot_general(
+        product[...] += lax.dot_general(
             xhi[:, cols], pieces, NT, preferred_element_type=f32
         ) + lax.dot_general(xlo[:, cols], pieces, NT, preferred_element_type=f32)
         add_gram(pieces)
@@ -243,18 +299,15 @@
     fold = product.shape[0] // 2
     last = ITERS
     for stage in range(ITERS):
-        def first_loop(k, carry, stage=stage):
+        product[...] = jnp.zeros_like(product)
+        gram_acc[...] = jnp.zeros_like(gram_acc)
+
+        def first_part(k, carry, stage=stage):
             chip_sum(k, stage == 0)
             copy_b(stage, k, k).start()
             return carry
 
-        lax.fori_loop(0, steps, first_loop, 0)
-        product[...] = jnp.zeros_like(product)
-        gram_acc[...] = jnp.zeros_like(gram_acc)
-        if stage > 0:
-            inverse[...] = inverse_factor(whole[stage - 1, fold : fold + rank // 2, :])
-
-        def second_loop(k, carry, stage=stage):
+        def second_part(k, carry, stage=stage):
             copy_b(stage, k, k).wait()
             value = send_b[k] + recv_b[stage, k]
             if stage > 0:
@@ -267,7 +320,16 @@
             add_product(recv_p[k], offset(k, 1 - core))
             return carry
 
-        lax.fori_loop(0, steps, second_loop, 0)
+        def both_parts(k, carry, stage=stage):
+            first_part(k, carry)
+            return second_part(k - lag, carry)
+
+        lag = min(2, steps)
+        lax.fori_loop(0, lag, first_part, 0)
+        if stage > 0:
+            inverse[...] = inverse_factor(whole[stage - 1, fold : fold + rank // 2, :])
+        lax.fori_loop(lag, steps, both_parts, 0)
+        lax.fori_loop(steps - lag, steps, second_part, 0)
 
         lane = lax.broadcasted_iota(jnp.int32, (fold, 2 * rank), 1)
         summed = product[...] + pltpu.roll(product[...], rank, 1)
@@ -316,9 +378,8 @@
             copy.wait()
         turned = whole[stage, 0:fold, :].T
         for part, rows in ((0, turned[0:rank]), (1, turned[rank:])):
-            width = min(fold, genes_dev - part * fold)
-            for i, piece in enumerate(split_three(rows[:, 0:width])):
-                wsplit[i * rank : (i + 1) * rank, part * fold : part * fold + width] = piece
+            for i, piece in enumerate(split_three(rows)):
+                wsplit[i * rank : (i + 1) * rank, part * fold : (part + 1) * fold] = piece
 
     def send_loop(j, carry):
         k = (1 - y) * per_quarter + j
@@ -394,15 +455,15 @@
     dma = pltpu.SemaphoreType.DMA
     scratch = [
         pltpu.VMEM((genes_dev, cells_dev), jnp.int32),
-        pltpu.VMEM((genes_dev, cells_dev), f32),
-        pltpu.VMEM((genes_dev, cells_dev), bf16),
-        pltpu.VMEM((genes_dev, cells_dev), bf16),
+        pltpu.VMEM((padded, cells_dev), f32),
+        pltpu.VMEM((padded, cells_dev), bf16),
+        pltpu.VMEM((padded, cells_dev), bf16),
         pltpu.VMEM((groups, 1, cells_dev), f32),
         pltpu.VMEM((padded, LANES), f32),
         pltpu.VMEM((padded, LANES), f32),
         pltpu.VMEM((padded, LANES), f32),
         pltpu.VMEM((half_devs, 8, padded), f32),
-        pltpu.VMEM((3 * rank, genes_dev), bf16),
+        pltpu.VMEM((3 * rank, padded), bf16),
         pltpu.VMEM((steps,) + block, f32),
         pltpu.VMEM((steps,) + block, f32),
         pltpu.VMEM((steps,) + block, f32),
@@ -446,7 +507,7 @@
             flops=flops, bytes_accessed=4 * genes_dev * cells_dev,
             transcendentals=genes_dev * cells_dev,
         ),
-    )(counts, start_basis.T)
+    )(counts, jnp.pad(start_basis, ((0, padded - genes_dev), (0, 0))).T)
     return turned.T
 
 

time: 130 us -> 119 us (0.915)
  Pallas kernels: 128 us -> 116 us
  local copies, waits for them, and re-layouts: 1.77 us -> 3.34 us
    pallas_call x1, Pallas kernels: 128 us -> 116 us  [shards(): pl.pallas_call(functools.partial(kernel, cfg), out_shape=jax.ShapeDtypeSt...]
    transpose x0 -> x1, local copies, waits for them, and re-layouts: none -> 1.57 us  [shards(): jnp.pad(start_basis, ((0, padded - genes_dev), (0, 0)))]
where the time goes in v2:
time: 119 us
  Pallas kernels  116 us (97%)
  local copies, waits for them, and re-layouts  3.34 us (3%)
    pallas_call x1, Pallas kernels, shards(): pl.pallas_call(functools.partial(kernel, cfg), out_shape=jax.ShapeDtypeSt...  116 us

profile of v2, /device:TPU:0, one launch (start us, length us, event | category | flops | bytes accessed | tf_op | source)
XLA Modules:
  0.0 119.3 jit_solution(8709944232836809222)
XLA Ops:
  0.0 1.6 %pad_bitcast_fusion.basis_ref = f32[64,512]{1,0:T(8,128)} fusion(f32[500,64]{0,1:T(8,128)} %param.3), kind=kLoop, calls=%fused_computation | loop fusion | bytes 259072 | tf_op jit(solution)/shard_map/transpose | solution.py:510
  1.6 115.9 %shard_map.28 = f32[64,1536]{1,0:T(8,128)} custom-call(s32[500,6144]{1,0:T(8,128)} %counts_ref.1, f32[64,512]{1,0:T(8,128)} %pad_bitcast_fusion.basis_ref), custom_call_target="tpu_custom_call" | custom-call | flops 7864320000 | bytes 12288000 | tf_op jit(solution)/shard_map/pallas_call | solution.py:497
  117.5 1.8 %copy.4 = f32[1536,64]{0,1:T(8,128)} copy(f32[1536,64]{0,1:T(8,128)} %bitcast.3) | data formatting | bytes 786432

commit v3 on v2

--- a/solution.py
+++ b/solution.py
@@ -32,14 +32,23 @@
     return high, middle, low
 
 
-def inverse_factor(gram_folded):
-    half_rows = gram_folded.shape[0]
-    rank = 2 * half_rows
+def elimination_grids(rank):
     lane = lax.broadcasted_iota(jnp.int32, (rank, 2 * rank), 1)
     row = lax.broadcasted_iota(jnp.int32, (rank, 2 * rank), 0)
+    return lane, row
+
+
+def elimination_start(gram_folded):
+    rank = 2 * gram_folded.shape[0]
+    lane, row = elimination_grids(rank)
+    gram = jnp.concatenate([gram_folded, pltpu.roll(gram_folded, rank, 1)], axis=0)
+    return jnp.where(lane < rank, gram, jnp.where(lane == row + rank, 1.0, 0.0))
+
+
+def elimination_run(both, first, stop):
+    rank = both.shape[0]
+    lane, row = elimination_grids(rank)
     row_column = lax.broadcasted_iota(jnp.int32, (rank, 1), 0)
-    gram = jnp.concatenate([gram_folded, pltpu.roll(gram_folded, rank, 1)], axis=0)
-    both = jnp.where(lane < rank, gram, jnp.where(lane == row + rank, 1.0, 0.0))
 
     def step(turn, both):
         k = turn * PIVOTS
@@ -67,17 +76,27 @@
             both = both - factor * rows[j]
         return both
 
-    both = lax.fori_loop(0, rank // PIVOTS, step, both)
+    return lax.fori_loop(first, stop, step, both)
+
+
+def elimination_end(both):
+    rank = both.shape[0]
+    lane, row = elimination_grids(rank)
     diagonal = jnp.sum(jnp.where(lane == row, both, 0.0), axis=1, keepdims=True)
     return both[:, rank:] * lax.rsqrt(diagonal)
+
+
+def inverse_factor(gram_folded):
+    both = elimination_start(gram_folded)
+    return elimination_end(elimination_run(both, 0, both.shape[0] // PIVOTS))
 
 
 def kernel(
     cfg, counts_ref, basis_ref, out_ref,
     cnt, logs, xhi, xlo, tot, acc, center_ref, scale_ref, stat, wsplit,
     send_a, recv_a, send_b, recv_b, own_p, recv_p, product, gram_acc, inverse,
-    shares, quarter_out, quarter_in, whole, gram_g, gram_c,
-    load_sem, tot_sem, stat_sem, a_sem, b_send, b_recv, c_sem, rs_sem, x_sem, ag_sem, gg_sem, gc_sem,
+    shares, quarter_out, quarter_in, whole, gram_in, gram_g, gram_c,
+    load_sem, tot_sem, stat_sem, a_sem, b_send, b_recv, c_sem, rs_sem, x_sem, ag_sem, gs_sem, gg_sem, gc_sem,
 ):
     genes_dev, cells_dev, rank, groups, cell_devs, chunk, share_rows = cfg
     half_devs = cell_devs // 2
@@ -92,7 +111,6 @@
     y_mate = {"genes": (1 - y) * 2 + core}
     dataset = cell // half_devs
     place = cell % half_devs
-    cross = {"cells": (1 - dataset) * half_devs + place}
 
     def gene_peer(i):
         return {"genes": (gene + i) % groups}
@@ -102,6 +120,9 @@
 
     def set_peer(i):
         return {"cells": dataset * half_devs + set_place(i)}
+
+    def cross_peer(i):
+        return {"cells": (1 - dataset) * half_devs + set_place(i)}
 
     def remote(src, dst, send, recv, device):
         return pltpu.make_async_remote_copy(
@@ -119,7 +140,8 @@
 
     barrier = pltpu.get_barrier_semaphore()
     mates = [gene_peer(i) for i in range(1, groups)]
-    mates += [set_peer(i) for i in range(1, half_devs)] + [cross]
+    mates += [set_peer(i) for i in range(1, half_devs)]
+    mates += [cross_peer(i) for i in range(half_devs)]
     for mate in mates:
         pl.semaphore_signal(barrier, inc=1, device_id=mate, device_id_type=pl.DeviceIdType.MESH)
 
@@ -326,19 +348,25 @@
 
         lag = min(2, steps)
         lax.fori_loop(0, lag, first_part, 0)
-        if stage > 0:
-            inverse[...] = inverse_factor(whole[stage - 1, fold : fold + rank // 2, :])
         lax.fori_loop(lag, steps, both_parts, 0)
         lax.fori_loop(steps - lag, steps, second_part, 0)
 
+        gram_acc[0 : rank // 2, :] = folded_gram()
+        gram_copies = [
+            remote(
+                gram_acc.at[0 : rank // 2], gram_in.at[stage, place],
+                gs_sem.at[0, stage, i], gs_sem.at[1, stage, i], cross_peer(i),
+            )
+            for i in range(half_devs)
+        ]
+        for copy in gram_copies:
+            copy.start()
         lane = lax.broadcasted_iota(jnp.int32, (fold, 2 * rank), 1)
         summed = product[...] + pltpu.roll(product[...], rank, 1)
         local = whole.at[ITERS + stage]
         local[0:fold, :] = jnp.where(lane < rank, summed[0:fold], summed[fold:])
-        local[fold : fold + rank // 2, :] = folded_gram()
-        if local.shape[0] > fold + rank // 2:
-            rest = local.shape[0] - fold - rank // 2
-            local[fold + rank // 2 :, :] = jnp.zeros((rest, 2 * rank), f32)
+        if local.shape[0] > fold:
+            local[fold:, :] = jnp.zeros((local.shape[0] - fold, 2 * rank), f32)
 
         def rows_of(index):
             return pl.ds(pl.multiple_of(index * share_rows, 8), share_rows)
@@ -359,9 +387,16 @@
             value = value + shares[stage, i]
         quarter_out[stage] = value
         copy = remote(
-            quarter_out.at[stage], quarter_in.at[stage], x_sem.at[0, stage], x_sem.at[1, stage], cross
+            quarter_out.at[stage], quarter_in.at[stage], x_sem.at[0, stage], x_sem.at[1, stage], cross_peer(0)
         )
         copy.start()
+        for gram_copy in gram_copies:
+            gram_copy.wait()
+        value = gram_in[stage, 0]
+        for i in range(1, half_devs):
+            value = value + gram_in[stage, i]
+        turns = rank // PIVOTS
+        both = elimination_run(elimination_start(value), 0, turns // 2)
         copy.wait()
         mine = rows_of(place)
         copies = [
@@ -374,6 +409,7 @@
         for copy in copies:
             copy.start()
         whole[stage, mine, :] = quarter_in[stage]
+        inverse[...] = elimination_end(elimination_run(both, turns // 2, turns))
         for copy in copies:
             copy.wait()
         turned = whole[stage, 0:fold, :].T
@@ -395,7 +431,6 @@
 
     lax.fori_loop(0, per_quarter, keep_loop, 0)
     gram_acc[...] = jnp.zeros_like(gram_acc)
-    inverse[...] = inverse_factor(whole[ITERS - 1, fold : fold + rank // 2, :])
 
     def last_loop(j, carry):
         copy_b(last, y * per_quarter + j, j).wait()
@@ -449,8 +484,7 @@
     chunk = max(c for c in range(LANES, 512 + 1, LANES) if quarter % c == 0)
     steps = 2 * quarter // chunk
     padded = -(-genes_dev // 256) * 256
-    rows = padded // 2 + rank // 2
-    share_rows = -(-rows // (8 * half_devs)) * 8
+    share_rows = -(-padded // 2 // (8 * half_devs)) * 8
     block = (rank, chunk)
     dma = pltpu.SemaphoreType.DMA
     scratch = [
@@ -477,6 +511,7 @@
         pltpu.VMEM((ITERS, share_rows, 2 * rank), f32),
         pltpu.VMEM((ITERS, share_rows, 2 * rank), f32),
         pltpu.VMEM((2 * ITERS, share_rows * half_devs, 2 * rank), f32),
+        pltpu.VMEM((ITERS, half_devs, rank // 2, 2 * rank), f32),
         pltpu.VMEM((groups, rank // 2, 2 * rank), f32),
         pltpu.VMEM((half_devs, rank // 2, 2 * rank), f32),
         dma((6,)),
@@ -488,6 +523,7 @@
         dma((2, steps)),
         dma((2, ITERS, half_devs)),
         dma((2, ITERS)),
+        dma((2, ITERS, half_devs)),
         dma((2, ITERS, half_devs)),
         dma((2, groups)),
         dma((2, half_devs)),

time: 119 us -> 119 us (level)
  no operation moved by 1% of the time
where the time goes in v3:
time: 119 us
  Pallas kernels  116 us (97%)
  local copies, waits for them, and re-layouts  3.34 us (3%)
    pallas_call x1, Pallas kernels, shards(): pl.pallas_call(functools.partial(kernel, cfg), out_shape=jax.ShapeDtypeSt...  116 us

profile of v3, /device:TPU:0, one launch (start us, length us, event | category | flops | bytes accessed | tf_op | source)
XLA Modules:
  0.0 118.9 jit_solution(14881886194247829926)
XLA Ops:
  0.0 1.6 %pad_bitcast_fusion.basis_ref = f32[64,512]{1,0:T(8,128)} fusion(f32[500,64]{0,1:T(8,128)} %param.3), kind=kLoop, calls=%fused_computation | loop fusion | bytes 259072 | tf_op jit(solution)/shard_map/transpose | solution.py:546
  1.6 115.6 %shard_map.28 = f32[64,1536]{1,0:T(8,128)} custom-call(s32[500,6144]{1,0:T(8,128)} %counts_ref.1, f32[64,512]{1,0:T(8,128)} %pad_bitcast_fusion.basis_ref), custom_call_target="tpu_custom_call" | custom-call | flops 7864320000 | bytes 12288000 | tf_op jit(solution)/shard_map/pallas_call | solution.py:533
  117.1 1.8 %copy.4 = f32[1536,64]{0,1:T(8,128)} copy(f32[1536,64]{0,1:T(8,128)} %bitcast.3) | data formatting | bytes 786432
